TPU v7x, 512 devices: a whole 4x8x8 slice. The times are simulated.
512 devices in a mesh: dp: 8 (over x, core), ctx: 64 (over y, z).
Axes of the slice: x: 4, y: 8, z: 8, core: 2. Of those that a mesh axis runs over, the one named last changes fastest.
Arguments:
- token_ids: int32 [8, 8192], P('dp', 'ctx'), may hold values from 0 to 7
- queries: bfloat16 [8, 8192, 4096], P('dp', 'ctx'), may hold values from -6 to 6
- gated_values: bfloat16 [8, 8192, 4096], P('dp', 'ctx'), may hold values from -6 to 6
- out_grad: bfloat16 [8, 8192, 4096], P('dp', 'ctx'), may hold values from -6 to 6
- filters: bfloat16 [4096, 128], P('ctx'), may hold values from -0.5 to 0.5
Outputs:
- value_grad: bfloat16 [8, 8192, 4096], P('dp', 'ctx')
- filter_grad: float32 [4096, 128], P('ctx')
Inputs may be any that keep to these rules, and one draw needn't show every extreme that they name: `token_ids`: ids 0 to 3 are upper-case bases, 4 to 7 lower-case bases.
All inputs are finite; a program needn't handle non-finite values.
Results may differ from a plain program's by a relative error of at most 0.0049.
Values may be sent and summed in bfloat16 or wider, within the bound.
A program may use at most 64 MiB of HBM per device.

v0:
```python
import jax
import jax.numpy as jnp
import numpy as np
from jax import lax
from jax.sharding import PartitionSpec as P


def tables(span):
    half = span // 2
    angle = np.pi * (2 * np.arange(half)[:, None] + 1) * np.arange(span)[None, :] / span
    wave = np.concatenate([np.cos(angle), np.sin(angle)], axis=0)
    high = wave.astype(jnp.bfloat16)
    low = (wave - high.astype(np.float64)).astype(jnp.bfloat16)
    return (high, low)


def mul(a, b):
    return jnp.dot(a, b, preferred_element_type=jnp.float32)


def body(token_ids, queries, gated_values, out_grad, filters):
    dp, ctx = (lax.axis_size("dp"), lax.axis_size("ctx"))
    weight = jnp.where(token_ids < 4, 1.0, 0.1).astype(jnp.float32)
    cotangent = (
        weight[:, :, None] * out_grad.astype(jnp.float32) * queries.astype(jnp.float32)
    ).astype(jnp.bfloat16)[0]
    rows = cotangent.shape[0]
    factor_tok = float(dp * ctx * rows) ** (-0.5)
    taps = lax.all_gather(filters, "ctx", axis=0, tiled=True)
    after = lax.ppermute(cotangent, "ctx", [(i, i - 1) for i in range(1, ctx)])
    high, low = (jnp.asarray(t) for t in tables(2 * rows))

    def forward(x):
        n = x.shape[0]
        wave = mul(high[:, :n], x) + mul(low[:, :n], x)
        return (wave[:rows], wave[rows:])

    def backward(re, im):
        both = jnp.concatenate([re, im], axis=0) * (1.0 / rows)
        top = both.astype(jnp.bfloat16)
        rest = (both - top.astype(jnp.float32)).astype(jnp.bfloat16)
        up, down = (high[:, :rows].T, low[:, :rows].T)
        return mul(up, top) + (mul(up, rest) + mul(down, top))

    cot_cos, cot_sin = forward(jnp.concatenate([cotangent, after], axis=0))

    def correlate(x):
        x_cos, x_sin = forward(x)
        return backward(cot_cos * x_cos + cot_sin * x_sin, cot_sin * x_cos - cot_cos * x_sin)

    tap_part = correlate(gated_values[0]).T * factor_tok
    filter_grad = lax.psum(lax.psum_scatter(tap_part, "ctx", scatter_dimension=0, tiled=True), "dp")
    value_grad = correlate(taps.T).astype(jnp.bfloat16)[None]
    return (value_grad, filter_grad)


def solution(mesh):
    return jax.shard_map(
        body,
        mesh=mesh,
        in_specs=(
            P("dp", "ctx"),
            P("dp", "ctx", None),
            P("dp", "ctx", None),
            P("dp", "ctx", None),
            P("ctx", None),
        ),
        out_specs=(P("dp", "ctx", None), P("ctx", None)),
        check_vma=False,
    )
```

profile of v0, /device:TPU:16, one launch (start us, length us, event | category | flops | bytes accessed | tf_op | source)
XLA Modules:
  0.0 386.2 jit_solution(3704554985823753769)
XLA Ops:
  7.2 0.0 copy-start
  7.2 0.0 copy-start.5
  7.2 0.0 all-gather.2.cloned.1.call-start
  7.2 0.7 all-gather.2.cloned.1.call-update
  7.9 0.0 reduce-scatter.2.cloned.1.call-start
  8.0 0.7 fusion.25
  8.6 1.9 fusion.13
  10.6 0.0 copy-start.4
  10.6 11.0 %collective-permute-start = (bf16[128,4096]{1,0:T(8,128)(2,1)S(1)}, bf16[128,4096]{1,0:T(8,128)(2,1)S(1)}, u32[]{:S(2)}, u32[]{:S(2)}) collective-permute-start(bf16[128,4096]{1,0:T(8,128)(2,1)S(1)} %fusion.13), channel_id=1, source_target_pairs={{1,0},{2,1},{3,2},{4,3},{5,4},{6,5},{7,6},{8,7},{9,8},{10,9},{11,1... | collective-permute-start | bytes 3145736 | tf_op jit(solution)/shard_map/ppermute | solution.py:30
  21.6 0.0 copy-done.5
  21.6 0.7 fusion.40
  22.3 0.0 copy-done.4
  22.3 0.7 fusion.39
  23.0 0.0 copy-done
  23.0 0.7 fusion.15
  23.7 0.0 copy-start.7
  23.7 2.7 convolution_add_fusion.2
  26.4 0.0 copy-start.6
  26.4 17.9 %collective-permute-done = bf16[128,4096]{1,0:T(8,128)(2,1)S(1)} collective-permute-done((bf16[128,4096]{1,0:T(8,128)(2,1)S(1)}, bf16[128,4096]{1,0:T(8,128)(2,1)S(1)}, u32[]{:S(2)}, u32[]{:S(2)}) %collective-permute-start) | collective-permute-done | bytes 1048608 | tf_op jit(solution)/shard_map/ppermute | solution.py:30
  44.3 0.0 copy-done.7
  44.3 0.7 convolution_add_fusion.1
  45.0 0.0 copy-done.6
  45.0 2.7 fusion.1
  47.7 49.9 %all-gather.2.cloned.1.call-done = bf16[4096,128]{1,0:T(8,128)(2,1)} async-done(((bf16[64,128]{1,0:T(8,128)(2,1)}), bf16[4096,128]{1,0:T(8,128)(2,1)}) %all-gather.2.cloned.1.call-update) | async-done | bytes 1048592 | tf_op jit(solution)/shard_map/all_gather | solution.py:29
  97.6 0.0 copy-start.3
  97.6 2.0 fusion.38
  99.6 0.0 copy-done.3
  99.6 0.0 copy-start.2
  99.6 2.7 convolution_add_fusion.3
  102.4 0.7 copy-done.2
  103.1 6.1 %multiply_add_fusion = (f32[128,4096]{1,0:T(8,128)S(1)}, f32[128,4096]{1,0:T(8,128)S(1)}, f32[128,4096]{1,0:T(8,128)S(1)}, f32[128,4096]{1,0:T(8,128)}) fusion(f32[256,4096]{1,0:T(8,128)S(1)} %copy-done.2, f32[256,4096]{1,0:T(8,128)} %fusion.1, f32[256,4096]{1,0:T(8,128)} %convolution_add_fusion.3), kind=kLoop, calls=%fused_computation.22 | loop fusion | flops 6291456 | bytes 20971520 | tf_op jit(solution)/shard_map/add | solution.py:49
  109.2 0.8 fusion.10
  110.0 0.8 fusion.23
  110.7 2.1 fusion.3
  112.8 0.0 reduce-scatter.2.cloned.1.call-update
  112.9 0.0 copy-start.1
  112.9 2.5 fusion.9
  115.4 0.0 copy-done.1
  115.4 0.8 fusion.19
  116.2 1.9 fusion.6
  118.1 2.3 copy.9
  120.4 234.3 %reduce-scatter.2.cloned.1.call-done = f32[64,128]{1,0:T(8,128)} async-done(((f32[4096,128]{1,0:T(8,128)}), f32[64,128]{1,0:T(8,128)}) %reduce-scatter.2.cloned.1.call-update) | async-done | bytes 32784 | tf_op jit(solution)/shard_map/reduce_scatter | solution.py:52
  354.7 24.7 %psum.7 = f32[64,128]{1,0:T(8,128)} all-reduce(f32[64,128]{1,0:T(8,128)} %reduce-scatter.2.cloned.1.call-done), channel_id=1, replica_groups=mesh['dp'=8,'ctx'=64] {'dp'}, use_global_device_ids=true, to_apply=%region_1.2 | all-reduce | flops 8192 | bytes 65536 | tf_op jit(solution)/shard_map/psum | solution.py:52
Async XLA Ops:
  7.2 15.8 %copy-start = (bf16[1,128,4096]{2,1,0:T(8,128)(2,1)S(1)}, bf16[1,128,4096]{2,1,0:T(8,128)(2,1)}, u32[]{:S(2)}) copy-start(bf16[1,128,4096]{2,1,0:T(8,128)(2,1)} %param.9) | copy-start | bytes 3145732
  7.2 14.4 %copy-start.5 = (bf16[256,128]{1,0:T(8,128)(2,1)S(1)}, bf16[256,128]{1,0:T(8,128)(2,1)}, u32[]{:S(2)}) copy-start(bf16[256,128]{1,0:T(8,128)(2,1)} %constant.22) | copy-start | bytes 196612
  7.2 90.4 %all-gather.2.cloned.1.call-start = ((), (), s32[]{:S(2)}) async-start(), calls=%async_computation.1 | async-start | bytes 1064960 | tf_op jit(solution)/shard_map/all_gather | solution.py:29
  7.9 346.8 %reduce-scatter.2.cloned.1.call-start = ((), (), s32[]{:S(2)}) async-start(), calls=%async_computation.2 | async-start | bytes 2129920 | tf_op jit(solution)/shard_map/reduce_scatter | solution.py:52
  10.6 11.7 %copy-start.4 = (bf16[256,128]{1,0:T(8,128)(2,1)S(1)}, bf16[256,128]{1,0:T(8,128)(2,1)}, u32[]{:S(2)}) copy-start(bf16[256,128]{1,0:T(8,128)(2,1)} %constant.20) | copy-start | bytes 196612
  10.6 33.7 %collective-permute-start = (bf16[128,4096]{1,0:T(8,128)(2,1)S(1)}, bf16[128,4096]{1,0:T(8,128)(2,1)S(1)}, u32[]{:S(2)}, u32[]{:S(2)}) collective-permute-start(bf16[128,4096]{1,0:T(8,128)(2,1)S(1)} %fusion.13), channel_id=1, source_target_pairs={{1,0},{2,1},{3,2},{4,3},{5,4},{6,5},{7,6},{8,7},{9,8},{10,9},{11,1... | collective-permute-start | bytes 3145736 | tf_op jit(solution)/shard_map/ppermute | solution.py:30
  23.7 20.6 %copy-start.7 = (bf16[256,128]{1,0:T(8,128)(2,1)S(1)}, bf16[256,128]{1,0:T(8,128)(2,1)}, u32[]{:S(2)}) copy-start(bf16[256,128]{1,0:T(8,128)(2,1)} %constant.21) | copy-start | bytes 196612
  26.4 18.6 %copy-start.6 = (bf16[256,128]{1,0:T(8,128)(2,1)S(1)}, bf16[256,128]{1,0:T(8,128)(2,1)}, u32[]{:S(2)}) copy-start(bf16[256,128]{1,0:T(8,128)(2,1)} %constant.23) | copy-start | bytes 196612
  97.6 2.0 copy-start.3
  99.6 3.5 copy-start.2
  112.9 2.5 copy-start.1
Sparse Core Ops, SparseCore 0:
  11.0 86.4 all-gather.1
  113.0 241.6 reduce-scatter.1
where the time goes:
time: 387 us; the launch traced here: 386 us
  waiting for transfers between devices  303 us (78%)
  blocking collectives  24.7 us (6%)
  matrix products  21.8 us (6%)
  between operations  14.2 us (4%)
  starting transfers between devices  11 us (3%)
  other arithmetic  8.73 us (2%)
    reduce_scatter x1, waiting for transfers between devices, body(): lax.psum_scatter(tap_part, 'ctx', scatter_dimension=0, tiled=True)  234 us
    all_gather x1, waiting for transfers between devices, body(): taps = lax.all_gather(filters, 'ctx', axis=0, tiled=True)  49.9 us
    psum x1, blocking collectives, body(): lax.psum(lax.psum_scatter(tap_part, 'ctx', scatter_dimension=0, tiled=Tru...  24.7 us
    dot_general x14, matrix products, mul(): return jnp.dot(a, b, preferred_element_type=jnp.float32)  21.8 us
    ppermute x1, waiting for transfers between devices, body(): after = lax.ppermute(cotangent, 'ctx', [(i, i - 1) for i in range(1, ctx)])  17.9 us
    ppermute x1, starting transfers between devices, body(): after = lax.ppermute(cotangent, 'ctx', [(i, i - 1) for i in range(1, ctx)])  11 us
  transfers between devices with their start and end apart: 3, of which 3 were waited for; matrix products, arithmetic and copies ran while one was open for 5% of the time, Pallas kernels for 0%

commit v1 on v0

--- a/solution.py
+++ b/solution.py
@@ -26,7 +26,9 @@
     ).astype(jnp.bfloat16)[0]
     rows = cotangent.shape[0]
     factor_tok = float(dp * ctx * rows) ** (-0.5)
-    taps = lax.all_gather(filters, "ctx", axis=0, tiled=True)
+    taps = jnp.concatenate(
+        lax.all_to_all(jnp.stack([filters] * lax.axis_size("ctx")), "ctx", 0, 0), axis=0
+    )
     after = lax.ppermute(cotangent, "ctx", [(i, i - 1) for i in range(1, ctx)])
     high, low = (jnp.asarray(t) for t in tables(2 * rows))
 

time: 387 us -> 366 us (0.946)
  waiting for transfers between devices: 303 us -> 272 us
  starting transfers between devices: 11 us -> 21.2 us
    all_gather x1 -> x0, waiting for transfers between devices: 49.9 us -> none  [body(): taps = lax.all_gather(filters, 'ctx', axis=0, tiled=True)]
    ppermute x1, waiting for transfers between devices: 17.9 us -> 35.1 us  [body(): after = lax.ppermute(cotangent, 'ctx', [(i, i - 1) for i in range(1, ctx)])]
    all_to_all x0 -> x1, starting transfers between devices: none -> 16.5 us  [body(): lax.all_to_all(jnp.stack([filters] * lax.axis_size('ctx')), 'ctx', 0, 0)]
    ppermute x1, starting transfers between devices: 11 us -> 4.71 us  [body(): after = lax.ppermute(cotangent, 'ctx', [(i, i - 1) for i in range(1, ctx)])]
  transfers between devices with their start and end apart: 3 -> 3, of which waited for: 3 -> 2; matrix products, arithmetic and copies ran while one was open for 5% -> 5% of each run, Pallas kernels for 0% -> 0%
where the time goes in v1:
time: 366 us; the launch traced here: 365 us
  waiting for transfers between devices  272 us (74%)
  blocking collectives  24.7 us (7%)
  starting transfers between devices  21.2 us (6%)
  matrix products  20.5 us (6%)
  between operations  14.2 us (4%)
  other arithmetic  7.79 us (2%)
  local copies, waits for them, and re-layouts  5.08 us (1%)
    reduce_scatter x1, waiting for transfers between devices, body(): lax.psum_scatter(tap_part, 'ctx', scatter_dimension=0, tiled=True)  237 us
    ppermute x1, waiting for transfers between devices, body(): after = lax.ppermute(cotangent, 'ctx', [(i, i - 1) for i in range(1, ctx)])  35.1 us
    psum x1, blocking collectives, body(): lax.psum(lax.psum_scatter(tap_part, 'ctx', scatter_dimension=0, tiled=Tru...  24.7 us
    dot_general x14, matrix products, mul(): return jnp.dot(a, b, preferred_element_type=jnp.float32)  20.5 us
    all_to_all x1, starting transfers between devices, body(): lax.all_to_all(jnp.stack([filters] * lax.axis_size('ctx')), 'ctx', 0, 0)  16.5 us
  transfers between devices with their start and end apart: 3, of which 2 were waited for; matrix products, arithmetic and copies ran while one was open for 5% of the time, Pallas kernels for 0%

profile of v1, /device:TPU:16, one launch (start us, length us, event | category | flops | bytes accessed | tf_op | source)
XLA Modules:
  0.0 365.5 jit_solution(6006528147043479035)
XLA Ops:
  7.2 0.0 copy-start
  7.2 0.0 copy-start.8
  7.2 0.0 copy-start.5
  7.2 2.1 stack.2
  9.3 16.5 %all-to-all-start = ((bf16[64,64,128]{2,1,0:T(8,128)(2,1)}), bf16[64,64,128]{2,1,0:T(8,128)(2,1)S(1)}, u32[]{:S(2)}, u32[]{:S(2)}) async-start(bf16[64,64,128]{2,1,0:T(8,128)(2,1)} %stack.2), calls=%async_computation | async-start | bytes 2097152 | tf_op jit(solution)/shard_map/all_to_all | solution.py:30
  25.8 0.0 copy-start.4
  25.8 0.0 reduce-scatter.2.cloned.1.call-start
  25.8 0.0 copy-done.8
  25.9 0.0 copy-done.5
  25.9 1.6 fusion.13
  27.5 0.0 copy-start.3
  27.5 4.7 %collective-permute-start = (bf16[128,4096]{1,0:T(8,128)(2,1)S(1)}, bf16[128,4096]{1,0:T(8,128)(2,1)S(1)}, u32[]{:S(2)}, u32[]{:S(2)}) collective-permute-start(bf16[128,4096]{1,0:T(8,128)(2,1)S(1)} %fusion.13), channel_id=1, source_target_pairs={{1,0},{2,1},{3,2},{4,3},{5,4},{6,5},{7,6},{8,7},{9,8},{10,9},{11,1... | collective-permute-start | bytes 3145736 | tf_op jit(solution)/shard_map/ppermute | solution.py:32
  32.2 0.0 copy-done.4
  32.2 0.7 fusion.40
  32.9 0.0 copy-done.3
  33.0 0.7 fusion.39
  33.7 0.0 copy-done
  33.7 0.7 fusion.15
  34.4 0.0 copy-start.7
  34.4 2.7 convolution_add_fusion.2
  37.1 0.0 copy-start.6
  37.1 35.1 %collective-permute-done = bf16[128,4096]{1,0:T(8,128)(2,1)S(1)} collective-permute-done((bf16[128,4096]{1,0:T(8,128)(2,1)S(1)}, bf16[128,4096]{1,0:T(8,128)(2,1)S(1)}, u32[]{:S(2)}, u32[]{:S(2)}) %collective-permute-start) | collective-permute-done | bytes 1048608 | tf_op jit(solution)/shard_map/ppermute | solution.py:32
  72.1 0.0 copy-done.7
  72.1 0.7 convolution_add_fusion.1
  72.9 0.0 copy-done.6
  72.9 2.7 fusion.1
  75.6 0.0 all-to-all-done
  75.6 0.7 fusion.38
  76.3 0.0 copy-start.2
  76.3 2.7 convolution_add_fusion.3
  79.0 0.7 copy-done.2
  79.7 6.2 %multiply_add_fusion = (f32[128,4096]{1,0:T(8,128)S(1)}, f32[128,4096]{1,0:T(8,128)S(1)}, f32[128,4096]{1,0:T(8,128)S(1)}, f32[128,4096]{1,0:T(8,128)}) fusion(f32[256,4096]{1,0:T(8,128)S(1)} %copy-done.2, f32[256,4096]{1,0:T(8,128)} %fusion.1, f32[256,4096]{1,0:T(8,128)} %convolution_add_fusion.3), kind=kLoop, calls=%fused_computation.22 | loop fusion | flops 6291456 | bytes 20971520 | tf_op jit(solution)/shard_map/add | solution.py:51
  85.9 0.8 fusion.10
  86.6 0.8 fusion.23
  87.4 2.1 fusion.3
  89.5 0.0 reduce-scatter.2.cloned.1.call-update
  89.5 0.0 copy-start.1
  89.5 2.5 fusion.9
  92.0 0.0 copy-done.1
  92.1 0.8 fusion.19
  92.9 1.9 fusion.6
  94.8 2.3 copy.9
  97.1 236.8 %reduce-scatter.2.cloned.1.call-done = f32[64,128]{1,0:T(8,128)} async-done(((f32[4096,128]{1,0:T(8,128)}), f32[64,128]{1,0:T(8,128)}) %reduce-scatter.2.cloned.1.call-update) | async-done | bytes 32784 | tf_op jit(solution)/shard_map/reduce_scatter | solution.py:54
  333.9 24.7 %psum.7 = f32[64,128]{1,0:T(8,128)} all-reduce(f32[64,128]{1,0:T(8,128)} %reduce-scatter.2.cloned.1.call-done), channel_id=1, replica_groups=mesh['dp'=8,'ctx'=64] {'dp'}, use_global_device_ids=true, to_apply=%region_1.2 | all-reduce | flops 8192 | bytes 65536 | tf_op jit(solution)/shard_map/psum | solution.py:54
  (1 shorter events, 0.0 us)
Async XLA Ops:
  7.2 26.5 %copy-start = (bf16[1,128,4096]{2,1,0:T(8,128)(2,1)S(1)}, bf16[1,128,4096]{2,1,0:T(8,128)(2,1)}, u32[]{:S(2)}) copy-start(bf16[1,128,4096]{2,1,0:T(8,128)(2,1)} %param.9) | copy-start | bytes 3145732
  7.2 18.7 %copy-start.8 = (s32[1,128]{1,0:T(1,128)S(1)}, s32[1,128]{1,0:T(1,128)}, u32[]{:S(2)}) copy-start(s32[1,128]{1,0:T(1,128)} %param.7) | copy-start | bytes 1540
  7.2 18.7 %copy-start.5 = (bf16[1,128,4096]{2,1,0:T(8,128)(2,1)S(1)}, bf16[1,128,4096]{2,1,0:T(8,128)(2,1)}, u32[]{:S(2)}) copy-start(bf16[1,128,4096]{2,1,0:T(8,128)(2,1)} %param.8) | copy-start | bytes 3145732
  9.3 66.3 %all-to-all-start = ((bf16[64,64,128]{2,1,0:T(8,128)(2,1)}), bf16[64,64,128]{2,1,0:T(8,128)(2,1)S(1)}, u32[]{:S(2)}, u32[]{:S(2)}) async-start(bf16[64,64,128]{2,1,0:T(8,128)(2,1)} %stack.2), calls=%async_computation | async-start | bytes 2097152 | tf_op jit(solution)/shard_map/all_to_all | solution.py:30
  25.8 6.5 %copy-start.4 = (bf16[256,128]{1,0:T(8,128)(2,1)S(1)}, bf16[256,128]{1,0:T(8,128)(2,1)}, u32[]{:S(2)}) copy-start(bf16[256,128]{1,0:T(8,128)(2,1)} %constant.22) | copy-start | bytes 196612
  25.8 308.1 %reduce-scatter.2.cloned.1.call-start = ((), (), s32[]{:S(2)}) async-start(), calls=%async_computation.2 | async-start | bytes 2129920 | tf_op jit(solution)/shard_map/reduce_scatter | solution.py:54
  27.5 5.4 %copy-start.3 = (bf16[256,128]{1,0:T(8,128)(2,1)S(1)}, bf16[256,128]{1,0:T(8,128)(2,1)}, u32[]{:S(2)}) copy-start(bf16[256,128]{1,0:T(8,128)(2,1)} %constant.20) | copy-start | bytes 196612
  27.5 44.6 %collective-permute-start = (bf16[128,4096]{1,0:T(8,128)(2,1)S(1)}, bf16[128,4096]{1,0:T(8,128)(2,1)S(1)}, u32[]{:S(2)}, u32[]{:S(2)}) collective-permute-start(bf16[128,4096]{1,0:T(8,128)(2,1)S(1)} %fusion.13), channel_id=1, source_target_pairs={{1,0},{2,1},{3,2},{4,3},{5,4},{6,5},{7,6},{8,7},{9,8},{10,9},{11,1... | collective-permute-start | bytes 3145736 | tf_op jit(solution)/shard_map/ppermute | solution.py:32
  34.4 37.8 %copy-start.7 = (bf16[256,128]{1,0:T(8,128)(2,1)S(1)}, bf16[256,128]{1,0:T(8,128)(2,1)}, u32[]{:S(2)}) copy-start(bf16[256,128]{1,0:T(8,128)(2,1)} %constant.21) | copy-start | bytes 196612
  37.1 35.8 %copy-start.6 = (bf16[256,128]{1,0:T(8,128)(2,1)S(1)}, bf16[256,128]{1,0:T(8,128)(2,1)}, u32[]{:S(2)}) copy-start(bf16[256,128]{1,0:T(8,128)(2,1)} %constant.23) | copy-start | bytes 196612
  76.3 3.4 copy-start.2
  89.5 2.5 copy-start.1
Sparse Core Ops, SparseCore 0:
  89.7 244.1 reduce-scatter.1
